TPU v7x, 32 devices: a whole 2x2x4 slice. The times are simulated.
32 devices in a mesh: curve: 8 (over z, y), slab: 4 (over x, core).
Axes of the slice: x: 2, y: 2, z: 4, core: 2. Of those that a mesh axis runs over, the one named last changes fastest.
Arguments:
- state: float32 [5, 125, 4, 1024], P(None, None, 'slab', 'curve'), as said below
- levels: int32 [4, 1024], P('slab', 'curve'), may hold values from 0 to 2
- neighbours: int32 [6, 4, 1024], P(None, 'slab', 'curve'), may hold values from 0 to 4095, as said below
- shifts: int32 [4, 8], P('slab', 'curve'), may hold values from -32 to 32
Outputs:
- moved: float32 [5, 125, 4, 1024], P(None, None, 'slab', 'curve')
- mortar: float32 [5, 25, 4, 1024], P(None, None, 'slab', 'curve')
Inputs may be any that keep to these rules, and one draw needn't show every extreme that they name: `neighbours`: faces 0 and 1 name an element of the row before and the row after (cyclically), faces 2 and 3 one of the same row; for faces 0 to 3 the named element sits in the same block of 128 positions; face 4 names one of the same row in the same block or the block before, face 5 in the same block or the block after (cyclically over blocks). `state`: density and pressure positive.
All inputs are finite; a program needn't handle non-finite values.
Results may differ from a plain program's by a relative error of at most 0.00021.
Values sent between devices are 32-bit elements; how exact they have to be, the bound alone decides.
A program may use at most 64 MiB of HBM per device.

v0:
```python
import jax
import jax.numpy as jnp
import numpy as np
from jax import lax
from jax.sharding import PartitionSpec as P

NV = 5
ORDER = 5
NODES = 125
FACE = 25


GAMMA = 1.4
CFL = 0.05
END_WEIGHT = 0.1


def padded(cells, sides, width):
    for axis, dim in sides:
        count = lax.axis_size(axis)
        head = lax.slice_in_dim(cells, 0, width, axis=dim)
        tail = lax.slice_in_dim(cells, cells.shape[dim] - width, cells.shape[dim], axis=dim)
        cells = jnp.concatenate(
            [
                lax.ppermute(tail, axis, [(i, (i + 1) % count) for i in range(count)]),
                cells,
                lax.ppermute(head, axis, [((i + 1) % count, i) for i in range(count)]),
            ],
            axis=dim,
        )
    return cells


def derivative_matrix():
    points = np.array([-1.0, -np.sqrt(3.0 / 7.0), 0.0, np.sqrt(3.0 / 7.0), 1.0])
    bary = np.array(
        [1.0 / np.prod([points[j] - points[k] for k in range(5) if k != j]) for j in range(5)]
    )
    table = np.zeros((5, 5))
    for i in range(5):
        for j in range(5):
            if i != j:
                table[i, j] = bary[j] / bary[i] / (points[i] - points[j])
        table[i, i] = -np.sum(table[i])
    return jnp.asarray(table, jnp.float32)


def euler_flux(u, d):
    density = u[0]
    momentum = u[1:4]
    energy = u[4]
    velocity = momentum / density
    press = (GAMMA - 1.0) * (energy - 0.5 * jnp.sum(momentum * velocity, axis=0))
    along = velocity[d]
    parts = [momentum[d]]
    for a in range(3):
        term = momentum[a] * along
        if a == d:
            term = term + press
        parts.append(term)
    parts.append((energy + press) * along)
    return jnp.stack(parts)


def wave_speed(u):
    velocity = u[1:4] / u[0]
    press = (GAMMA - 1.0) * (u[4] - 0.5 * jnp.sum(u[1:4] * velocity, axis=0))
    return jnp.sqrt(jnp.sum(velocity * velocity, axis=0)) + jnp.sqrt(GAMMA * press / u[0])


def rusanov(lower, upper, d, lam):
    return 0.5 * (euler_flux(lower, d) + euler_flux(upper, d)) - 0.5 * lam * (upper - lower)


def own_faces(u5):
    return [u5[:, :, :, 0], u5[:, :, :, 4], u5[:, :, 0], u5[:, :, 4], u5[:, 0], u5[:, 4]]


def onehot(axis, index):
    shape = [1, 1, 1, 1, 1]
    shape[axis] = 5
    return (jnp.arange(5) == index).astype(jnp.float32).reshape(shape)


def residual(u5, outer, scale, lam):
    table = derivative_matrix()
    high = lax.Precision.HIGHEST
    div = jnp.einsum("ai,vkjie->vkjae", table, euler_flux(u5, 0), precision=high)
    div = div + jnp.einsum("aj,vkjie->vkaie", table, euler_flux(u5, 1), precision=high)
    div = div + jnp.einsum("ak,vkjie->vajie", table, euler_flux(u5, 2), precision=high)
    faces = own_faces(u5)
    correct = jnp.zeros_like(u5)
    for d in range(3):
        axis = 3 - d
        inner_low = faces[2 * d]
        inner_high = faces[2 * d + 1]
        lift_low = (
            rusanov(outer[2 * d], inner_low, d, lam) - euler_flux(inner_low, d)
        ) / END_WEIGHT
        lift_high = (
            rusanov(inner_high, outer[2 * d + 1], d, lam) - euler_flux(inner_high, d)
        ) / END_WEIGHT
        correct = correct + jnp.expand_dims(lift_low, axis) * onehot(axis, 0)
        correct = correct - jnp.expand_dims(lift_high, axis) * onehot(axis, 4)
    return scale * (correct - div)


def on_device(state, levels, neighbours, shifts):
    count = state.shape[-1]
    u5 = state.reshape(NV, ORDER, ORDER, ORDER, count)
    scale = jnp.exp2(levels.reshape(count).astype(jnp.float32))
    speed = wave_speed(u5)
    lam, top = lax.pmax((jnp.max(speed), jnp.max(speed * scale)), ("curve", "slab"))
    faces = own_faces(u5)
    grid = jnp.stack([jnp.stack([faces[0], faces[5]]), jnp.stack([faces[4], faces[1]])])
    extended = padded(grid, (("curve", 1), ("slab", 0)), 1)
    below_x, above_x = (extended[0, 2], extended[3, 1])
    below_z, above_z = (extended[1, 0], extended[2, 3])
    local = neighbours.reshape(6, count)
    offset = local % count
    mine = lax.axis_index("curve")
    elsewhere = (local // count % lax.axis_size("curve") != mine).astype(jnp.int32) * count
    slot = offset + elsewhere
    outer = [
        jnp.take(below_x, offset[0], axis=-1),
        jnp.take(above_x, offset[1], axis=-1),
        jnp.take(faces[3], offset[2], axis=-1),
        jnp.take(faces[2], offset[3], axis=-1),
        jnp.take(jnp.concatenate([faces[5], below_z], axis=-1), slot[4], axis=-1),
        jnp.take(jnp.concatenate([faces[4], above_z], axis=-1), slot[5], axis=-1),
    ]
    new = u5 + CFL / top * residual(u5, outer, scale, lam)
    most = count // 4
    moved_by = shifts.reshape(())
    width = most + 1
    window = padded(new, (("curve", 4),), width)
    start = width + moved_by
    upper = window[:, 4]
    before = lax.dynamic_slice_in_dim(upper, start - 1, count, 3)
    moved_block = lax.dynamic_slice_in_dim(window, start, count, 4)
    mflux = rusanov(before, moved_block[:, 0], 2, lam)
    moved = moved_block.reshape(NV, NODES, 1, count)
    mortar = mflux.reshape(NV, FACE, 1, count)
    return (moved, mortar)


def solution(mesh):
    placed = (
        P(None, None, "slab", "curve"),
        P("slab", "curve"),
        P(None, "slab", "curve"),
        P("slab", "curve"),
    )
    return jax.shard_map(
        on_device,
        mesh=mesh,
        in_specs=placed,
        out_specs=(P(None, None, "slab", "curve"), P(None, None, "slab", "curve")),
        check_vma=False,
    )
```

profile of v0, /device:TPU:0, one launch (start us, length us, event | category | flops | bytes accessed | tf_op | source)
XLA Modules:
  0.0 150.9 jit_solution(3773034216713242610)
XLA Ops:
  0.6 1.8 %reduce.4 = f32[5,125,128]{2,1,0:T(8,128)S(1)} reduce(f32[5,125,1,128]{3,2,1,0:T(1,128)} %param.9, f32[]{:T(128)} %constant.120), dimensions={2}, to_apply=%param.9.reduce_sub_computation | reduce | bytes 640004 | tf_op args[0]
  4.2 3.0 %collective-permute-start = (f32[2,1,5,5,5,128]{5,4,3,2,1,0:T(8,128)}, f32[2,1,5,5,5,128]{5,4,3,2,1,0:T(8,128)}, u32[]{:S(2)}, u32[]{:S(2)}) collective-permute-start(f32[2,1,5,5,5,128]{5,4,3,2,1,0:T(8,128)} %get-tuple-element.105), channel_id=1, source_target_pairs={{0,4},{4,8},{8,12},{12,16},{16,20},{20,24},{24,28},{28,0},{1,5},{5... | collective-permute-start | bytes 384008 | tf_op jit(solution)/shard_map/ppermute | solution.py:25
  7.2 3.0 %collective-permute-start.1 = (f32[2,1,5,5,5,128]{5,4,3,2,1,0:T(8,128)}, f32[2,1,5,5,5,128]{5,4,3,2,1,0:T(8,128)}, u32[]{:S(2)}, u32[]{:S(2)}) collective-permute-start(f32[2,1,5,5,5,128]{5,4,3,2,1,0:T(8,128)} %get-tuple-element.106), channel_id=1, source_target_pairs={{4,0},{8,4},{12,8},{16,12},{20,16},{24,20},{28,24},{0,28},{5,1},{9... | collective-permute-start | bytes 384008 | tf_op jit(solution)/shard_map/ppermute | solution.py:27
  21.1 1.7 %copy.105 = f32[5,5,5,128]{2,1,3,0:T(8,128)S(1)} copy(f32[5,5,5,128]{3,2,1,0:T(8,128)} %get-tuple-element.75) | data formatting | bytes 128000 | tf_op jit(solution)/shard_map/squeeze | solution.py:76
  23.5 2.4 %gather_fusion.3 = f32[128,5,5,5]{3,2,1,0:T(8,128)} fusion(f32[5,5,5,128]{2,1,3,0:T(8,128)S(1)} %copy.105, s32[1024]{0:T(1024)S(1)} %pad_clamp_fusion.2), kind=kCustom, calls=%fused_computation.4.clone | custom fusion | bytes 128512 | tf_op jit(solution)/shard_map/jit(_take)/gather | solution.py:128
  25.8 2.2 %copy.106 = f32[128,5,5,5]{0,3,2,1:T(8,128)S(1)} copy(f32[128,5,5,5]{3,2,1,0:T(8,128)} %gather_fusion.3) | data formatting | bytes 128000 | tf_op jit(solution)/shard_map/jit(_take)/gather | solution.py:128
  29.3 1.7 %copy.92 = f32[5,5,5,128]{2,1,3,0:T(8,128)S(1)} copy(f32[5,5,5,128]{3,2,1,0:T(8,128)} %get-tuple-element.74) | data formatting | bytes 128000 | tf_op jit(solution)/shard_map/squeeze | solution.py:76
  31.7 2.4 %gather_fusion.2 = f32[128,5,5,5]{3,2,1,0:T(8,128)} fusion(f32[5,5,5,128]{2,1,3,0:T(8,128)S(1)} %copy.92, s32[1024]{0:T(1024)S(1)} %pad_clamp_fusion.3), kind=kCustom, calls=%fused_computation.3.clone | custom fusion | bytes 128512 | tf_op jit(solution)/shard_map/jit(_take)/gather | solution.py:127
  34.1 2.3 %copy.93 = f32[128,5,5,5]{0,3,2,1:T(8,128)S(1)} copy(f32[128,5,5,5]{3,2,1,0:T(8,128)} %gather_fusion.2) | data formatting | bytes 128000 | tf_op jit(solution)/shard_map/jit(_take)/gather | solution.py:127
  42.3 38.2 %all-reduce = (f32[]{:T(128)}, f32[]{:T(128)}) all-reduce(f32[]{:T(128)} %get-tuple-element.12, f32[]{:T(128)} %get-tuple-element.11), channel_id=1, replica_groups=mesh['curve'=8,'slab'=4] {'curve','slab'}, use_global_device_ids=true, to_apply=%region_7.9 | all-reduce | flops 2 | bytes 16 | tf_op jit(solution)/shard_map/pmax | solution.py:113
  84.5 1.7 %collective-permute-start.3 = (f32[1,4,5,5,5,128]{5,4,3,2,1,0:T(8,128)}, f32[1,4,5,5,5,128]{5,4,3,2,1,0:T(8,128)}, u32[]{:S(2)}, u32[]{:S(2)}) collective-permute-start(f32[1,4,5,5,5,128]{5,4,3,2,1,0:T(8,128)} %get-tuple-element.55), channel_id=1, source_target_pairs={{1,0},{2,1},{3,2},{0,3},{5,4},{6,5},{7,6},{4,7},{9,8},{10,9},{11,1... | collective-permute-start | bytes 768008 | tf_op jit(solution)/shard_map/ppermute | solution.py:27
  87.2 3.1 %copy.111 = f32[5,5,5,256]{2,1,3,0:T(8,128)} copy(f32[5,5,5,256]{3,2,1,0:T(8,128)S(1)} %pad_maximum_fusion.4) | data formatting | bytes 256000 | tf_op jit(solution)/shard_map/concatenate | solution.py:130
  90.3 3.5 %gather_fusion.5 = f32[128,5,5,5]{3,2,1,0:T(8,128)S(1)} fusion(f32[5,5,5,256]{2,1,3,0:T(8,128)} %copy.111, s32[1024]{0:T(1024)} %pad_clamp_fusion), kind=kCustom, calls=%fused_computation.5.clone | custom fusion | bytes 128512 | tf_op jit(solution)/shard_map/jit(_take)/gather | solution.py:130
  95.6 3.1 %copy.107 = f32[5,5,5,256]{2,1,3,0:T(8,128)} copy(f32[5,5,5,256]{3,2,1,0:T(8,128)S(1)} %pad_maximum_fusion.3) | data formatting | bytes 256000 | tf_op jit(solution)/shard_map/concatenate | solution.py:129
  98.7 3.5 %gather_fusion.4 = f32[128,5,5,5]{3,2,1,0:T(8,128)S(1)} fusion(f32[5,5,5,256]{2,1,3,0:T(8,128)} %copy.107, s32[1024]{0:T(1024)} %pad_clamp_fusion.1), kind=kCustom, calls=%fused_computation.1.clone | custom fusion | bytes 128512 | tf_op jit(solution)/shard_map/jit(_take)/gather | solution.py:129
  103.5 2.1 %subtract_multiply_fusion.3 = (f32[5,5,5,128]{3,2,1,0:T(8,128)}, f32[5,5,5,128]{3,2,1,0:T(8,128)}, f32[5,5,5,128]{3,2,1,0:T(8,128)}, f32[5,5,5,128]{3,2,1,0:T(8,128)}) fusion(f32[5,5,5,128]{3,2,1,0:T(8,128)} %copy-done.39, f32[5,5,5,128]{3,2,1,0:T(8,128)} %copy-done.41, f32[]{:T(128)S(6)} %mul.994, f32[5,5,5,5,128]{4,3,2,1,0:T(8,128)S(1)} %reshape.830, ...), kind=kLoop, calls=%fused_computation.161 | loop fusion | flops 512000 | bytes 1280516 | tf_op jit(solution)/shard_map/div | solution.py:97
  107.4 2.4 %gather_fusion = f32[128,5,5,5]{3,2,1,0:T(8,128)} fusion(f32[5,5,5,128]{2,1,3,0:T(8,128)S(1)} %copy.77, s32[1024]{0:T(1024)S(1)} %pad_clamp_fusion.5), kind=kCustom, calls=%fused_computation.clone | custom fusion | bytes 128512 | tf_op jit(solution)/shard_map/jit(_take)/gather | solution.py:125
  109.7 2.2 %copy.78 = f32[128,5,5,5]{0,3,2,1:T(8,128)S(1)} copy(f32[128,5,5,5]{3,2,1,0:T(8,128)} %gather_fusion) | data formatting | bytes 128000 | tf_op jit(solution)/shard_map/jit(_take)/gather | solution.py:125
  114.6 2.4 %gather_fusion.1 = f32[128,5,5,5]{3,2,1,0:T(8,128)} fusion(f32[5,5,5,128]{2,1,3,0:T(8,128)S(1)} %copy.89, s32[1024]{0:T(1024)S(1)} %pad_clamp_fusion.4), kind=kCustom, calls=%fused_computation.2.clone | custom fusion | bytes 128512 | tf_op jit(solution)/shard_map/jit(_take)/gather | solution.py:126
  117.0 2.4 %copy.90 = f32[128,5,5,5]{0,3,2,1:T(8,128)S(1)} copy(f32[128,5,5,5]{3,2,1,0:T(8,128)} %gather_fusion.1) | data formatting | bytes 128000 | tf_op jit(solution)/shard_map/jit(_take)/gather | solution.py:126
  120.9 2.5 %collective-permute-start.4 = (f32[5,5,5,5,33]{4,3,2,1,0:T(8,128)S(1)}, f32[5,5,5,5,33]{4,3,2,1,0:T(8,128)S(1)}, u32[]{:S(2)}, u32[]{:S(2)}) collective-permute-start(f32[5,5,5,5,33]{4,3,2,1,0:T(8,128)S(1)} %get-tuple-element.56), channel_id=1, source_target_pairs={{0,4},{4,8},{8,12},{12,16},{16,20},{20,24},{24,28},{28,0},{1,5},{5... | collective-permute-start | bytes 247508 | tf_op jit(solution)/shard_map/ppermute | solution.py:25
  123.4 2.3 %collective-permute-start.5 = (f32[5,5,5,5,33]{4,3,2,1,0:T(8,128)S(1)}, f32[5,5,5,5,33]{4,3,2,1,0:T(8,128)S(1)}, u32[]{:S(2)}, u32[]{:S(2)}) collective-permute-start(f32[5,5,5,5,33]{4,3,2,1,0:T(8,128)S(1)} %get-tuple-element.57), channel_id=1, source_target_pairs={{4,0},{8,4},{12,8},{16,12},{20,16},{24,20},{28,24},{0,28},{5,1},{9... | collective-permute-start | bytes 247508 | tf_op jit(solution)/shard_map/ppermute | solution.py:27
  126.4 18.8 %collective-permute-done.4 = f32[5,5,5,5,33]{4,3,2,1,0:T(8,128)S(1)} collective-permute-done((f32[5,5,5,5,33]{4,3,2,1,0:T(8,128)S(1)}, f32[5,5,5,5,33]{4,3,2,1,0:T(8,128)S(1)}, u32[]{:S(2)}, u32[]{:S(2)}) %collective-permute-start.4) | collective-permute-done | bytes 82532 | tf_op jit(solution)/shard_map/ppermute | solution.py:25
  145.2 2.2 %collective-permute-done.5 = f32[5,5,5,5,33]{4,3,2,1,0:T(8,128)S(1)} collective-permute-done((f32[5,5,5,5,33]{4,3,2,1,0:T(8,128)S(1)}, f32[5,5,5,5,33]{4,3,2,1,0:T(8,128)S(1)}, u32[]{:S(2)}, u32[]{:S(2)}) %collective-permute-start.5) | collective-permute-done | bytes 82532 | tf_op jit(solution)/shard_map/ppermute | solution.py:27
  (303 shorter events, 35.9 us)
Async XLA Ops:
  0.6 11.0 %copy-start = (f32[5,125,1,128]{3,2,1,0:T(1,128)S(1)}, f32[5,125,1,128]{3,2,1,0:T(1,128)}, u32[]{:S(2)}) copy-start(f32[5,125,1,128]{3,2,1,0:T(1,128)} %param.9) | copy-start | bytes 960004
  2.4 10.7 %copy-start.66 = (s32[6,1,128]{2,1,0:T(1,128)S(1)}, s32[6,1,128]{2,1,0:T(1,128)}, u32[]{:S(2)}) copy-start(s32[6,1,128]{2,1,0:T(1,128)} %param.11) | copy-start | bytes 9220
  3.2 15.2 %copy-start.70 = (s32[1,128]{1,0:T(1,128)S(1)}, s32[1,128]{1,0:T(1,128)}, u32[]{:S(2)}) copy-start(s32[1,128]{1,0:T(1,128)} %param.10) | copy-start | bytes 1540
  3.3 7.6 %copy-start.16 = (f32[5,5,5,1,128]{4,3,2,1,0:T(1,128)}, f32[5,5,5,1,128]{4,3,2,1,0:T(1,128)S(1)}, u32[]{:S(2)}) copy-start(f32[5,5,5,1,128]{4,3,2,1,0:T(1,128)S(1)} %get-tuple-element.95) | copy-start | bytes 192004
  3.3 8.4 %copy-start.18 = (f32[5,5,5,1,128]{4,3,2,1,0:T(1,128)}, f32[5,5,5,1,128]{4,3,2,1,0:T(1,128)S(1)}, u32[]{:S(2)}) copy-start(f32[5,5,5,1,128]{4,3,2,1,0:T(1,128)S(1)} %get-tuple-element.94) | copy-start | bytes 192004
  4.2 78.2 %collective-permute-start = (f32[2,1,5,5,5,128]{5,4,3,2,1,0:T(8,128)}, f32[2,1,5,5,5,128]{5,4,3,2,1,0:T(8,128)}, u32[]{:S(2)}, u32[]{:S(2)}) collective-permute-start(f32[2,1,5,5,5,128]{5,4,3,2,1,0:T(8,128)} %get-tuple-element.105), channel_id=1, source_target_pairs={{0,4},{4,8},{8,12},{12,16},{16,20},{20,24},{24,28},{28,0},{1,5},{5... | collective-permute-start | bytes 384008 | tf_op jit(solution)/shard_map/ppermute | solution.py:25
  7.2 75.2 %collective-permute-start.1 = (f32[2,1,5,5,5,128]{5,4,3,2,1,0:T(8,128)}, f32[2,1,5,5,5,128]{5,4,3,2,1,0:T(8,128)}, u32[]{:S(2)}, u32[]{:S(2)}) collective-permute-start(f32[2,1,5,5,5,128]{5,4,3,2,1,0:T(8,128)} %get-tuple-element.106), channel_id=1, source_target_pairs={{4,0},{8,4},{12,8},{16,12},{20,16},{24,20},{28,24},{0,28},{5,1},{9... | collective-permute-start | bytes 384008 | tf_op jit(solution)/shard_map/ppermute | solution.py:27
  10.9 5.2 %copy-start.48 = (f32[1,5,5,1,128]{4,3,2,1,0:T(1,128)}, f32[1,5,5,1,128]{4,3,2,1,0:T(1,128)S(1)}, u32[]{:S(2)}) copy-start(f32[1,5,5,1,128]{4,3,2,1,0:T(1,128)S(1)} %get-tuple-element.64) | copy-start | bytes 38404
  10.9 5.2 %copy-start.50 = (f32[1,5,5,1,128]{4,3,2,1,0:T(1,128)}, f32[1,5,5,1,128]{4,3,2,1,0:T(1,128)S(1)}, u32[]{:S(2)}) copy-start(f32[1,5,5,1,128]{4,3,2,1,0:T(1,128)S(1)} %get-tuple-element.61) | copy-start | bytes 38404
  12.4 7.5 %copy-start.13 = (f32[1,125,1,128]{3,2,1,0:T(1,128)}, f32[1,125,1,128]{3,2,1,0:T(1,128)S(1)}, u32[]{:S(2)}) copy-start(f32[1,125,1,128]{3,2,1,0:T(1,128)S(1)} %get-tuple-element.115) | copy-start | bytes 192004
  37.7 44.0 %copy-start.69 = (s32[128]{0:T(128)S(1)}, s32[128]{0:T(128)}, u32[]{:S(2)}) copy-start(s32[128]{0:T(128)} %get-tuple-element.42) | copy-start | bytes 1540
  37.9 46.6 %copy-start.11 = (f32[5,5,5,5,128]{4,3,2,1,0:T(8,128)}, f32[5,5,5,5,128]{4,3,2,1,0:T(8,128)S(1)}, u32[]{:S(2)}) copy-start(f32[5,5,5,5,128]{4,3,2,1,0:T(8,128)S(1)} %get-tuple-element.101) | copy-start | bytes 960004
  39.4 47.8 %copy-start.21 = (f32[5,5,5,128]{3,2,1,0:T(8,128)S(1)}, f32[5,5,5,128]{3,2,1,0:T(8,128)}, u32[]{:S(2)}) copy-start(f32[5,5,5,128]{3,2,1,0:T(8,128)} %get-tuple-element.93) | copy-start | bytes 192004
  41.0 46.1 %copy-start.32 = (f32[5,5,5,128]{3,2,1,0:T(8,128)}, f32[5,5,5,128]{3,2,1,0:T(8,128)S(1)}, u32[]{:S(2)}) copy-start(f32[5,5,5,128]{3,2,1,0:T(8,128)S(1)} %get-tuple-element.165) | copy-start | bytes 192004
  41.1 46.1 %copy-start.35 = (f32[5,5,5,128]{3,2,1,0:T(8,128)}, f32[5,5,5,128]{3,2,1,0:T(8,128)S(1)}, u32[]{:S(2)}) copy-start(f32[5,5,5,128]{3,2,1,0:T(8,128)S(1)} %get-tuple-element.166) | copy-start | bytes 192004
  84.5 21.1 %collective-permute-start.2 = (f32[1,4,5,5,5,128]{5,4,3,2,1,0:T(8,128)}, f32[1,4,5,5,5,128]{5,4,3,2,1,0:T(8,128)}, u32[]{:S(2)}, u32[]{:S(2)}) collective-permute-start(f32[1,4,5,5,5,128]{5,4,3,2,1,0:T(8,128)} %get-tuple-element.54), channel_id=1, source_target_pairs={{0,1},{1,2},{2,3},{3,0},{4,5},{5,6},{6,7},{7,4},{8,9},{9,10},{10,1... | collective-permute-start | bytes 768008 | tf_op jit(solution)/shard_map/ppermute | solution.py:25
  84.5 27.6 %collective-permute-start.3 = (f32[1,4,5,5,5,128]{5,4,3,2,1,0:T(8,128)}, f32[1,4,5,5,5,128]{5,4,3,2,1,0:T(8,128)}, u32[]{:S(2)}, u32[]{:S(2)}) collective-permute-start(f32[1,4,5,5,5,128]{5,4,3,2,1,0:T(8,128)} %get-tuple-element.55), channel_id=1, source_target_pairs={{1,0},{2,1},{3,2},{0,3},{5,4},{6,5},{7,6},{4,7},{9,8},{10,9},{11,1... | collective-permute-start | bytes 768008 | tf_op jit(solution)/shard_map/ppermute | solution.py:27
  90.3 5.2 %copy-start.20 = (f32[5,5,5,128]{3,2,1,0:T(8,128)S(1)}, f32[5,5,5,128]{3,2,1,0:T(8,128)}, u32[]{:S(2)}) copy-start(f32[5,5,5,128]{3,2,1,0:T(8,128)} %get-tuple-element.90) | copy-start | bytes 192004
  106.5 5.5 %copy-start.62 = (pred[128]{0:T(512)(128)(4,1)S(1)}, pred[128]{0:T(512)(128)(4,1)}, u32[]{:S(2)}) copy-start(pred[128]{0:T(512)(128)(4,1)} %get-tuple-element.161) | copy-start | bytes 388
  113.7 5.7 %copy-start.61 = (pred[128]{0:T(512)(128)(4,1)S(1)}, pred[128]{0:T(512)(128)(4,1)}, u32[]{:S(2)}) copy-start(pred[128]{0:T(512)(128)(4,1)} %get-tuple-element.155) | copy-start | bytes 388
  113.7 5.9 %copy-start.19 = (f32[5,5,5,1,128]{4,3,2,1,0:T(1,128)S(1)}, f32[5,5,5,1,128]{4,3,2,1,0:T(1,128)}, u32[]{:S(2)}) copy-start(f32[5,5,5,1,128]{4,3,2,1,0:T(1,128)} %copy-done.18) | copy-start | bytes 192004
  114.5 5.1 %copy-start.23 = (f32[5,5,5,128]{3,2,1,0:T(8,128)S(1)}, f32[5,5,5,128]{3,2,1,0:T(8,128)}, u32[]{:S(2)}) copy-start(f32[5,5,5,128]{3,2,1,0:T(8,128)} %get-tuple-element.70) | copy-start | bytes 192004
  120.9 24.3 %collective-permute-start.4 = (f32[5,5,5,5,33]{4,3,2,1,0:T(8,128)S(1)}, f32[5,5,5,5,33]{4,3,2,1,0:T(8,128)S(1)}, u32[]{:S(2)}, u32[]{:S(2)}) collective-permute-start(f32[5,5,5,5,33]{4,3,2,1,0:T(8,128)S(1)} %get-tuple-element.56), channel_id=1, source_target_pairs={{0,4},{4,8},{8,12},{12,16},{16,20},{20,24},{24,28},{28,0},{1,5},{5... | collective-permute-start | bytes 247508 | tf_op jit(solution)/shard_map/ppermute | solution.py:25
  123.4 24.0 %collective-permute-start.5 = (f32[5,5,5,5,33]{4,3,2,1,0:T(8,128)S(1)}, f32[5,5,5,5,33]{4,3,2,1,0:T(8,128)S(1)}, u32[]{:S(2)}, u32[]{:S(2)}) collective-permute-start(f32[5,5,5,5,33]{4,3,2,1,0:T(8,128)S(1)} %get-tuple-element.57), channel_id=1, source_target_pairs={{4,0},{8,4},{12,8},{16,12},{20,16},{24,20},{28,24},{0,28},{5,1},{9... | collective-permute-start | bytes 247508 | tf_op jit(solution)/shard_map/ppermute | solution.py:27
  (53 other events, 149.8 us)
where the time goes:
time: 152 us; the launch traced here: 151 us
  local copies, waits for them, and re-layouts  55.5 us (37%)
  blocking collectives  38.2 us (25%)
  waiting for transfers between devices  21 us (14%)
  other arithmetic  15.8 us (10%)
  starting transfers between devices  12.5 us (8%)
  between operations  4.07 us (3%)
  matrix products  3.73 us (2%)
    pmax x1, blocking collectives, on_device(): lax.pmax((jnp.max(speed), jnp.max(speed * scale)), ('curve', 'slab'))  38.2 us
    ppermute x3, waiting for transfers between devices, padded(): lax.ppermute(tail, axis, [(i, (i + 1) % count) for i in range(count)])  18.8 us
    ppermute x3, starting transfers between devices, padded(): lax.ppermute(head, axis, [((i + 1) % count, i) for i in range(count)])  7.06 us
    unnamed x159, local copies, waits for them, and re-layouts  6.43 us
    ppermute x3, starting transfers between devices, padded(): lax.ppermute(tail, axis, [(i, (i + 1) % count) for i in range(count)])  5.48 us
    gather x2, local copies, waits for them, and re-layouts, on_device(): jnp.take(above_x, offset[1], axis=-1)  4.74 us
    gather x2, local copies, waits for them, and re-layouts, on_device(): jnp.take(faces[3], offset[2], axis=-1)  4.69 us
    gather x2, local copies, waits for them, and re-layouts, on_device(): jnp.take(below_x, offset[0], axis=-1)  4.59 us
  transfers between devices with their start and end apart: 6, of which 2 were waited for; matrix products, arithmetic and copies ran while one was open for 36% of the time, Pallas kernels for 0%

commit v1 on v0

v1 whole, which is shorter than its diff:
```python
import functools

import jax
import jax.numpy as jnp
import ml_dtypes
import numpy as np
from jax import lax
from jax.experimental import pallas as pl
from jax.experimental.pallas import tpu as pltpu
from jax.sharding import PartitionSpec as P

NV = 5
ORDER = 5
NODES = 125
FACE = 25
NPAD = 128
FPAD = 32

GAMMA = 1.4
CFL = 0.05
END_WEIGHT = 0.1
BF16 = jnp.bfloat16
F32 = jnp.float32


def derivative_matrix():
    points = np.array([-1.0, -np.sqrt(3.0 / 7.0), 0.0, np.sqrt(3.0 / 7.0), 1.0])
    bary = np.array(
        [1.0 / np.prod([points[j] - points[k] for k in range(5) if k != j]) for j in range(5)]
    )
    table = np.zeros((5, 5))
    for i in range(5):
        for j in range(5):
            if i != j:
                table[i, j] = bary[j] / bary[i] / (points[i] - points[j])
        table[i, i] = -np.sum(table[i])
    return np.asarray(table, np.float32)


def face_nodes():
    n = np.arange(NODES).reshape(5, 5, 5)
    return [
        n[:, :, 0], n[:, :, 4], n[:, 0, :], n[:, 4, :], n[0], n[4],
    ]


def matrices():
    table = derivative_matrix()
    eye = np.eye(5, dtype=np.float32)
    per_dim = [
        np.kron(np.kron(eye, eye), table),
        np.kron(np.kron(eye, table), eye),
        np.kron(np.kron(table, eye), eye),
    ]
    wide = np.zeros((NPAD, 3 * NPAD), np.float32)
    for d in range(3):
        wide[:NODES, d * NPAD : d * NPAD + NODES] = -per_dim[d]
    high = wide.astype(ml_dtypes.bfloat16)
    low = (wide - high.astype(np.float32)).astype(ml_dtypes.bfloat16)
    signed = np.zeros((NPAD, 6 * FPAD), np.float32)
    plain = np.zeros((NPAD, 6 * FPAD), np.float32)
    half = 0.5 / END_WEIGHT
    for f, nodes in enumerate(face_nodes()):
        for r, n in enumerate(nodes.reshape(-1)):
            signed[n, f * FPAD + r] = half if f % 2 == 0 else -half
            plain[n, f * FPAD + r] = half
    div = np.concatenate([high, high, low], axis=1)
    signed = np.concatenate([signed, signed], axis=1).astype(ml_dtypes.bfloat16)
    plain = np.concatenate([plain, plain], axis=1).astype(ml_dtypes.bfloat16)
    return div, signed, plain


def primitive(u):
    inv = 1.0 / u[0]
    vel = [u[1] * inv, u[2] * inv, u[3] * inv]
    kinetic = u[1] * vel[0] + u[2] * vel[1] + u[3] * vel[2]
    press = (GAMMA - 1.0) * (u[4] - 0.5 * kinetic)
    return inv, vel, press


def flux(u, vel, press, d):
    along = vel[d]
    parts = [u[1 + d]]
    for a in range(3):
        term = u[1 + a] * along
        parts.append(term + press if a == d else term)
    parts.append((u[4] + press) * along)
    return parts


def flux_of(u, d):
    _, vel, press = primitive(u)
    return flux(u, vel, press, d)


def split(x, parts):
    out = []
    for p in range(parts):
        piece = x.astype(BF16)
        out.append(piece)
        if p < parts - 1:
            x = x - piece.astype(F32)
    return out


def mm(a, b):
    return jnp.dot(a, b, preferred_element_type=F32)


def pick(x, chosen):
    rows = x.shape[0]
    y = mm(jnp.concatenate(split(x, 3), axis=0), chosen)
    return y[:rows] + y[rows : 2 * rows] + y[2 * rows :]


def one_hot(rows, index):
    where = lax.broadcasted_iota(jnp.int32, (rows, index.shape[1]), 0)
    return jnp.where(where == index, 1.0, 0.0).astype(BF16)


def kernel(
    n_curve, n_slab,
    state_ref, ints_ref, div_ref, signed_ref, plain_ref,
    moved_ref, mortar_ref,
    faces, got, mine_s, mine_c, from_s, from_c, head, tail, got_head, got_tail, upper_ref,
    face_send, face_recv, s_send, s_recv, c_send, c_recv, halo_send, halo_recv,
):
    count = state_ref.shape[2]
    width = count // 4
    curve = lax.axis_index("curve")
    slab = lax.axis_index("slab")

    def on_curve(t):
        return {"curve": lax.rem(curve + t + n_curve, n_curve)}

    def on_slab(t):
        return {"slab": lax.rem(slab + t + n_slab, n_slab)}

    def remote(src, dst, send, recv, to):
        return pltpu.make_async_remote_copy(
            src_ref=src, dst_ref=dst, send_sem=send, recv_sem=recv,
            device_id=to, device_id_type=pl.DeviceIdType.MESH,
        )

    barrier = pltpu.get_barrier_semaphore()
    for t in range(1, n_slab):
        pl.semaphore_signal(barrier, inc=1, device_id=on_slab(t), device_id_type=pl.DeviceIdType.MESH)
    for t in range(1, n_curve):
        pl.semaphore_signal(barrier, inc=1, device_id=on_curve(t), device_id_type=pl.DeviceIdType.MESH)

    ones = jnp.ones((8, count), F32)
    for f in range(6):
        for v in range(NV):
            r = v * FPAD
            faces[f, r + 24 : r + 32, :] = ones
            if f < 2:
                faces[f, r : r + FACE, :] = state_ref[v, pl.ds(4 * f, FACE, stride=5), :]
            elif f < 4:
                for k in range(5):
                    n = 25 * k + 20 * (f - 2)
                    faces[f, r + 5 * k : r + 5 * k + 5, :] = state_ref[v, n : n + 5, :]
            else:
                n = 100 * (f - 4)
                faces[f, r : r + FACE, :] = state_ref[v, n : n + FACE, :]

    ints = ints_ref[...]
    scale = jnp.exp2(ints[6:7].astype(F32))
    u = [state_ref[v] for v in range(NV)]
    inv, vel, press = primitive(u)
    speed = jnp.sqrt(vel[0] * vel[0] + vel[1] * vel[1] + vel[2] * vel[2]) + jnp.sqrt(GAMMA * press * inv)
    node = lax.broadcasted_iota(jnp.int32, speed.shape, 0)
    fastest = jnp.max(jnp.where(node < NODES, speed, 0.0), axis=0, keepdims=True)
    row8 = lax.broadcasted_iota(jnp.int32, (8, count), 0)
    mine_s[...] = jnp.where(row8 == 0, fastest, fastest * scale)

    pl.semaphore_wait(barrier, n_slab + n_curve - 2)
    copies_s = []
    for t in range(1, n_slab):
        c = remote(mine_s, from_s.at[t - 1], s_send.at[t - 1], s_recv.at[t - 1], on_slab(t))
        c.start()
        copies_s.append(c)
    copies_f = [
        remote(faces.at[5], got.at[2], face_send.at[2], face_recv.at[2], on_curve(1)),
        remote(faces.at[4], got.at[3], face_send.at[3], face_recv.at[3], on_curve(-1)),
        remote(faces.at[1], got.at[0], face_send.at[0], face_recv.at[0], on_slab(1)),
        remote(faces.at[0], got.at[1], face_send.at[1], face_recv.at[1], on_slab(-1)),
    ]
    for c in copies_f:
        c.start()

    blocks = []
    for d in range(3):
        blocks.append(jnp.concatenate(flux(u, vel, press, d), axis=1))
    whole = jnp.concatenate(blocks, axis=0)
    whole_high, whole_low = split(whole, 2)

    for c in copies_s:
        c.wait()
    best = mine_s[...]
    for t in range(n_slab - 1):
        best = jnp.maximum(best, from_s[t])
    mine_c[...] = best
    copies_c = []
    for t in range(1, n_curve):
        c = remote(mine_c, from_c.at[t - 1], c_send.at[t - 1], c_recv.at[t - 1], on_curve(t))
        c.start()
        copies_c.append(c)

    total = mm(div_ref[...], jnp.concatenate([whole_high, whole_low, whole_high], axis=0))

    jumps, diffs = [None] * 6, [None] * 6

    def lift(f, outer):
        d = f // 2
        a = [faces[f, v * FPAD : (v + 1) * FPAD, :] for v in range(NV)]
        b = [outer[v * FPAD : (v + 1) * FPAD] for v in range(NV)]
        fa, fb = flux_of(a, d), flux_of(b, d)
        diffs[f] = jnp.concatenate([y - x for x, y in zip(fa, fb)], axis=1)
        jumps[f] = jnp.concatenate([y - x for x, y in zip(a, b)], axis=1)

    lift(2, pick(faces[3], one_hot(count, ints[2:3])))
    lift(3, pick(faces[2], one_hot(count, ints[3:4])))
    for g, f in ((0, 0), (1, 1)):
        copies_f[2 + g].wait()
        lift(f, pick(got[g], one_hot(count, ints[f : f + 1])))
    for g, f in ((2, 4), (3, 5)):
        copies_f[g - 2].wait()
        pair = jnp.concatenate([faces[9 - f], got[g]], axis=1)
        lift(f, pick(pair, one_hot(2 * count, ints[f : f + 1])))

    diff_all = jnp.concatenate(diffs, axis=0)
    jump_all = jnp.concatenate(jumps, axis=0)
    total = total + mm(signed_ref[...], jnp.concatenate(split(diff_all, 2), axis=0))
    spread = mm(plain_ref[...], jnp.concatenate(split(jump_all, 2), axis=0))

    for c in copies_c:
        c.wait()
    for t in range(n_curve - 1):
        best = jnp.maximum(best, from_c[t])
    peak = jnp.max(best, axis=1, keepdims=True)
    lam = peak[0:1]
    step = scale * (CFL / peak[1:2])

    lane = lax.broadcasted_iota(jnp.int32, (1, count), 1)
    part = lane // width
    new = []
    extra = jnp.zeros((FPAD, count), F32)
    for v in range(NV):
        cols = slice(v * count, (v + 1) * count)
        x = u[v] + step * (total[:, cols] + lam * spread[:, cols])
        new.append(x)
        packed_head, packed_tail = x[:FPAD], x[:FPAD]
        for g in range(1, 4):
            turned = pltpu.roll(x[g * FPAD : (g + 1) * FPAD], g * width, 1)
            packed_head = jnp.where(part == g, turned, packed_head)
            packed_tail = jnp.where(part == (3 + g) % 4, turned, packed_tail)
        head[v * FPAD : (v + 1) * FPAD, :] = packed_head
        tail[v * FPAD : (v + 1) * FPAD, :] = packed_tail
        last = pltpu.roll(x[3 * FPAD :], (v - (count - width - 1)) % count, 1)
        extra = jnp.where(lane == v, last, extra)
    tail[NV * FPAD :, :] = extra
    halo = [
        remote(tail, got_tail, halo_send.at[0], halo_recv.at[0], on_curve(1)),
        remote(head, got_head, halo_send.at[1], halo_recv.at[1], on_curve(-1)),
    ]
    for c in halo:
        c.start()

    shift = ints[7:8]

    def chosen(start):
        q = start + lane
        q = jnp.where(q < 0, q + count, jnp.where(q >= count, q - count, q))
        return one_hot(count, q), (lane < start) | (lane >= count + start)

    hot, foreign = chosen(shift)
    hot_before, foreign_before = chosen(shift - 1)
    for c in halo:
        c.wait()

    rows, rows_before = [], []
    extra = got_tail[NV * FPAD :, :]
    for v in range(NV):
        below = got_tail[v * FPAD : (v + 1) * FPAD, :]
        above = got_head[v * FPAD : (v + 1) * FPAD, :]
        for g in range(4):
            ends = jnp.where(part == g, above, below)
            if g:
                ends = pltpu.roll(ends, count - g * width, 1)
            own = new[v][g * FPAD : (g + 1) * FPAD]
            rows.append(jnp.where(foreign, ends, own))
        last = pltpu.roll(extra, count - width - 1 - v, 1)
        ends = jnp.where(lane == count - width - 1, last, ends)
        rows_before.append(jnp.where(foreign_before, ends, own))
    out = pick(jnp.concatenate(rows, axis=0), hot)
    for v in range(NV):
        moved_ref[v] = out[v * NPAD : v * NPAD + NODES]
    upper_ref[...] = pick(jnp.concatenate(rows_before, axis=0), hot_before)

    skip = NODES - FACE - 3 * FPAD
    lower = [upper_ref[v * FPAD + skip : v * FPAD + skip + FACE, :] for v in range(NV)]
    upper = [moved_ref[v, 0:FACE, :] for v in range(NV)]
    fl, fu = flux_of(lower, 2), flux_of(upper, 2)
    for v in range(NV):
        mortar_ref[v] = 0.5 * (fl[v] + fu[v]) - 0.5 * lam * (upper[v] - lower[v])


def on_device(n_curve, n_slab, state, levels, neighbours, shifts):
    count = state.shape[-1]
    padded = jnp.pad(
        state.reshape(NV, NODES, count), ((0, 0), (0, NPAD - NODES), (0, 0)), constant_values=1.0
    )
    local = neighbours.reshape(6, count)
    elsewhere = (local // count % n_curve != lax.axis_index("curve")).astype(jnp.int32) * count
    face = jnp.arange(6, dtype=jnp.int32)[:, None]
    slot = local % count + jnp.where(face >= 4, elsewhere, 0)
    ints = jnp.concatenate(
        [slot, levels.reshape(1, count), jnp.broadcast_to(shifts.reshape(1, 1), (1, count))], axis=0
    )
    div, signed, plain = matrices()
    vmem = pl.BlockSpec(memory_space=pltpu.VMEM)
    moved, mortar = pl.pallas_call(
        functools.partial(kernel, n_curve, n_slab),
        out_shape=(
            jax.ShapeDtypeStruct((NV, NODES, count), F32),
            jax.ShapeDtypeStruct((NV, FACE, count), F32),
        ),
        in_specs=[vmem] * 5,
        out_specs=(vmem, vmem),
        scratch_shapes=[
            pltpu.VMEM((6, NV * FPAD, count), F32),
            pltpu.VMEM((4, NV * FPAD, count), F32),
            pltpu.VMEM((8, count), F32),
            pltpu.VMEM((8, count), F32),
            pltpu.VMEM((n_slab - 1, 8, count), F32),
            pltpu.VMEM((n_curve - 1, 8, count), F32),
            pltpu.VMEM((NV * FPAD, count), F32),
            pltpu.VMEM((NV * FPAD + FPAD, count), F32),
            pltpu.VMEM((NV * FPAD, count), F32),
            pltpu.VMEM((NV * FPAD + FPAD, count), F32),
            pltpu.VMEM((NV * FPAD, count), F32),
            pltpu.SemaphoreType.DMA((4,)),
            pltpu.SemaphoreType.DMA((4,)),
            pltpu.SemaphoreType.DMA((n_slab - 1,)),
            pltpu.SemaphoreType.DMA((n_slab - 1,)),
            pltpu.SemaphoreType.DMA((n_curve - 1,)),
            pltpu.SemaphoreType.DMA((n_curve - 1,)),
            pltpu.SemaphoreType.DMA((2,)),
            pltpu.SemaphoreType.DMA((2,)),
        ],
        compiler_params=pltpu.CompilerParams(
            collective_id=0, has_side_effects=True, vmem_limit_bytes=32 * 1024 * 1024
        ),
        name="substep",
    )(padded, ints, jnp.asarray(div), jnp.asarray(signed), jnp.asarray(plain))
    return moved.reshape(NV, NODES, 1, count), mortar.reshape(NV, FACE, 1, count)


def solution(mesh):
    placed = (
        P(None, None, "slab", "curve"),
        P("slab", "curve"),
        P(None, "slab", "curve"),
        P("slab", "curve"),
    )
    return jax.shard_map(
        functools.partial(on_device, mesh.shape["curve"], mesh.shape["slab"]),
        mesh=mesh,
        in_specs=placed,
        out_specs=(P(None, None, "slab", "curve"), P(None, None, "slab", "curve")),
        check_vma=False,
    )
```

time: 152 us -> 25.9 us (0.17)
  local copies, waits for them, and re-layouts: 55.5 us -> 4.99 us
  blocking collectives: 38.2 us -> 0 us
  waiting for transfers between devices: 21 us -> 0 us
  Pallas kernels: 0 us -> 19.2 us
  other arithmetic: 15.8 us -> 0.15 us
  starting transfers between devices: 12.5 us -> 0 us
  matrix products: 3.73 us -> 0 us
  between operations: 4.07 us -> 1.34 us
    pmax x1 -> x0, blocking collectives: 38.2 us -> none  [on_device(): lax.pmax((jnp.max(speed), jnp.max(speed * scale)), ('curve', 'slab'))]
    gather x12 -> x0, local copies, waits for them, and re-layouts: 26.8 us -> none  [the longest x2 4.74 us: on_device(): jnp.take(above_x, offset[1], axis=-1)]
    ppermute x6 -> x0, waiting for transfers between devices: 21 us -> none  [the longest x3 18.8 us: padded(): lax.ppermute(tail, axis, [(i, (i + 1) % count) for i in range(count)])]
    pallas_call x0 -> x1, Pallas kernels: none -> 19.2 us  [on_device(): pl.pallas_call(functools.partial(kernel, n_curve, n_slab), out_shape=(jax...]
    ppermute x6 -> x0, starting transfers between devices: 12.5 us -> none  [the longest x3 7.06 us: padded(): lax.ppermute(head, axis, [((i + 1) % count, i) for i in range(count)])]
    squeeze x10 -> x0, local copies, waits for them, and re-layouts: 10.2 us -> none  [the longest x4 3.53 us: on_device(): below_x, above_x = (extended[0, 2], extended[3, 1])]
    concatenate x2 -> x1, local copies, waits for them, and re-layouts: 6.23 us -> 0.07 us  [on_device(): jnp.concatenate([slot, levels.reshape(1, count), jnp.broadcast_to(shifts....]
    dot_general x3 -> x0, matrix products: 3.73 us -> none  [the longest x1 1.41 us: residual(): jnp.einsum('ak,vkjie->vajie', table, euler_flux(u5, 2), precision=high)]
  transfers between devices with their start and end apart: 6 -> 0, of which waited for: 2 -> 0; matrix products, arithmetic and copies ran while one was open for 36% -> 0% of each run, Pallas kernels for 0% -> 0%
where the time goes in v1:
time: 25.9 us; the launch traced here: 25.7 us
  Pallas kernels  19.2 us (74%)
  local copies, waits for them, and re-layouts  4.99 us (19%)
  between operations  1.34 us (5%)
    pallas_call x1, Pallas kernels, on_device(): pl.pallas_call(functools.partial(kernel, n_curve, n_slab), out_shape=(jax...  19.2 us
    unnamed x13, local copies, waits for them, and re-layouts  4.89 us

profile of v1, /device:TPU:0, one launch (start us, length us, event | category | flops | bytes accessed | tf_op | source)
XLA Modules:
  0.0 25.7 jit_solution(7576122189388126461)
XLA Ops:
  1.3 0.0 copy-start.3
  1.3 0.1 pad.7.clone
  1.4 0.6 %copy-done.3 = s32[6,1,128]{2,1,0:T(1,128)S(1)} copy-done((s32[6,1,128]{2,1,0:T(1,128)S(1)}, s32[6,1,128]{2,1,0:T(1,128)}, u32[]{:S(2)}) %copy-start.3) | copy-done | bytes 3096
  2.0 0.0 copy-start.4
  2.0 0.1 fusion
  2.0 0.6 %copy-done.4 = s32[1,128]{1,0:T(1,128)S(1)} copy-done((s32[1,128]{1,0:T(1,128)S(1)}, s32[1,128]{1,0:T(1,128)}, u32[]{:S(2)}) %copy-start.4) | copy-done | bytes 536
  2.6 0.1 add_add_fusion.ints_ref
  2.7 1.0 %copy.31 = f32[5,125,1,128]{3,1,2,0:T(8,128)S(1)} copy(f32[5,125,1,128]{3,2,1,0:T(1,128)} %param.7) | data formatting | bytes 640000
  3.7 0.0 copy-start
  3.7 0.0 copy-start.1
  3.7 0.0 copy-start.2
  3.8 0.9 %copy-done = bf16[128,1152]{1,0:T(8,128)(2,1)S(1)} copy-done((bf16[128,1152]{1,0:T(8,128)(2,1)S(1)}, bf16[128,1152]{1,0:T(8,128)(2,1)}, u32[]{:S(2)}) %copy-start) | copy-done | bytes 294936
  4.7 0.0 copy-done.1
  4.7 0.0 copy-done.2
  4.7 19.2 %substep.1 = (f32[5,125,128]{2,1,0:T(8,128)S(1)}, f32[5,25,128]{2,1,0:T(8,128)S(1)}) custom-call(f32[5,128,128]{2,1,0:T(8,128)S(1)} %pad.4.state_ref, s32[8,128]{1,0:T(8,128)S(1)} %add_add_fusion.ints_ref, bf16[128,1152]{1,0:T(8,128)(2,1)S(1)} %copy-done, bf16[128,384]{1,0:T(8,128)(2,1)S(1)} %copy-done.2, bf16[128,384]{1,0:T(8,128)(2,1)S(1)} %copy-done.1), custom_call_target="tpu_custom_call" | custom-call | tf_op jit(solution)/shard_map/substep/pallas_call | solution.py:322
  23.9 1.1 %copy.9 = f32[5,125,1,128]{3,2,1,0:T(1,128)} copy(f32[5,125,1,128]{3,1,0,2:T(8,128)S(1)} %bitcast.27) | data formatting | bytes 640000
  25.0 0.7 %copy.10 = f32[5,25,1,128]{3,2,1,0:T(1,128)} copy(f32[5,25,1,128]{3,1,0,2:T(8,128)S(1)} %bitcast.28) | data formatting | bytes 128000
  (2 shorter events, 0.0 us)
Async XLA Ops:
  1.3 0.7 %copy-start.3 = (s32[6,1,128]{2,1,0:T(1,128)S(1)}, s32[6,1,128]{2,1,0:T(1,128)}, u32[]{:S(2)}) copy-start(s32[6,1,128]{2,1,0:T(1,128)} %param.9) | copy-start | bytes 9220
  2.0 0.7 %copy-start.4 = (s32[1,128]{1,0:T(1,128)S(1)}, s32[1,128]{1,0:T(1,128)}, u32[]{:S(2)}) copy-start(s32[1,128]{1,0:T(1,128)} %param.8) | copy-start | bytes 1540
  3.7 1.0 %copy-start = (bf16[128,1152]{1,0:T(8,128)(2,1)S(1)}, bf16[128,1152]{1,0:T(8,128)(2,1)}, u32[]{:S(2)}) copy-start(bf16[128,1152]{1,0:T(8,128)(2,1)} %constant.57.clone.div_ref) | copy-start | bytes 884740
  3.7 1.0 %copy-start.1 = (bf16[128,384]{1,0:T(8,128)(2,1)S(1)}, bf16[128,384]{1,0:T(8,128)(2,1)}, u32[]{:S(2)}) copy-start(bf16[128,384]{1,0:T(8,128)(2,1)} %constant.59.clone.plain_ref) | copy-start | bytes 294916
  3.7 1.0 %copy-start.2 = (bf16[128,384]{1,0:T(8,128)(2,1)S(1)}, bf16[128,384]{1,0:T(8,128)(2,1)}, u32[]{:S(2)}) copy-start(bf16[128,384]{1,0:T(8,128)(2,1)} %constant.58.clone.signed_ref) | copy-start | bytes 294916

commit v2 on v1

--- a/solution.py
+++ b/solution.py
@@ -58,16 +58,11 @@
     high = wide.astype(ml_dtypes.bfloat16)
     low = (wide - high.astype(np.float32)).astype(ml_dtypes.bfloat16)
     signed = np.zeros((NPAD, 6 * FPAD), np.float32)
-    plain = np.zeros((NPAD, 6 * FPAD), np.float32)
     half = 0.5 / END_WEIGHT
     for f, nodes in enumerate(face_nodes()):
         for r, n in enumerate(nodes.reshape(-1)):
             signed[n, f * FPAD + r] = half if f % 2 == 0 else -half
-            plain[n, f * FPAD + r] = half
-    div = np.concatenate([high, high, low], axis=1)
-    signed = np.concatenate([signed, signed], axis=1).astype(ml_dtypes.bfloat16)
-    plain = np.concatenate([plain, plain], axis=1).astype(ml_dtypes.bfloat16)
-    return div, signed, plain
+    return np.concatenate([high, low], axis=1), signed.astype(ml_dtypes.bfloat16)
 
 
 def primitive(u):
@@ -120,7 +115,7 @@
 
 def kernel(
     n_curve, n_slab,
-    state_ref, ints_ref, div_ref, signed_ref, plain_ref,
+    state_ref, levels_ref, neighbours_ref, shifts_ref, div_ref, signed_ref,
     moved_ref, mortar_ref,
     faces, got, mine_s, mine_c, from_s, from_c, head, tail, got_head, got_tail, upper_ref,
     face_send, face_recv, s_send, s_recv, c_send, c_recv, halo_send, halo_recv,
@@ -163,13 +158,12 @@
                 n = 100 * (f - 4)
                 faces[f, r : r + FACE, :] = state_ref[v, n : n + FACE, :]
 
-    ints = ints_ref[...]
-    scale = jnp.exp2(ints[6:7].astype(F32))
     u = [state_ref[v] for v in range(NV)]
     inv, vel, press = primitive(u)
     speed = jnp.sqrt(vel[0] * vel[0] + vel[1] * vel[1] + vel[2] * vel[2]) + jnp.sqrt(GAMMA * press * inv)
     node = lax.broadcasted_iota(jnp.int32, speed.shape, 0)
     fastest = jnp.max(jnp.where(node < NODES, speed, 0.0), axis=0, keepdims=True)
+    scale = jnp.exp2(levels_ref[...].astype(F32))
     row8 = lax.broadcasted_iota(jnp.int32, (8, count), 0)
     mine_s[...] = jnp.where(row8 == 0, fastest, fastest * scale)
 
@@ -206,7 +200,8 @@
         c.start()
         copies_c.append(c)
 
-    total = mm(div_ref[...], jnp.concatenate([whole_high, whole_low, whole_high], axis=0))
+    total = mm(div_ref[...], jnp.concatenate([whole_high, whole_high], axis=0))
+    total = total + mm(div_ref[:, : 3 * NPAD], whole_low)
 
     jumps, diffs = [None] * 6, [None] * 6
 
@@ -218,20 +213,31 @@
         diffs[f] = jnp.concatenate([y - x for x, y in zip(fa, fb)], axis=1)
         jumps[f] = jnp.concatenate([y - x for x, y in zip(a, b)], axis=1)
 
-    lift(2, pick(faces[3], one_hot(count, ints[2:3])))
-    lift(3, pick(faces[2], one_hot(count, ints[3:4])))
-    for g, f in ((0, 0), (1, 1)):
+    def first(t_slab, t_curve):
+        row = lax.rem(slab + t_slab + n_slab, n_slab)
+        return (row * n_curve + lax.rem(curve + t_curve + n_curve, n_curve)) * count
+
+    lift(2, pick(faces[3], one_hot(count, neighbours_ref[2] - first(0, 0))))
+    lift(3, pick(faces[2], one_hot(count, neighbours_ref[3] - first(0, 0))))
+    for g, t in ((0, -1), (1, 1)):
+        hot = one_hot(count, neighbours_ref[g] - first(t, 0))
         copies_f[2 + g].wait()
-        lift(f, pick(got[g], one_hot(count, ints[f : f + 1])))
-    for g, f in ((2, 4), (3, 5)):
+        lift(g, pick(got[g], hot))
+    for g, f, t in ((2, 4, -1), (3, 5, 1)):
+        near = one_hot(count, neighbours_ref[f] - first(0, 0))
+        far = one_hot(count, neighbours_ref[f] - first(0, t))
+        hot = jnp.concatenate([near, far], axis=0)
         copies_f[g - 2].wait()
-        pair = jnp.concatenate([faces[9 - f], got[g]], axis=1)
-        lift(f, pick(pair, one_hot(2 * count, ints[f : f + 1])))
+        lift(f, pick(jnp.concatenate([faces[9 - f], got[g]], axis=1), hot))
 
     diff_all = jnp.concatenate(diffs, axis=0)
     jump_all = jnp.concatenate(jumps, axis=0)
-    total = total + mm(signed_ref[...], jnp.concatenate(split(diff_all, 2), axis=0))
-    spread = mm(plain_ref[...], jnp.concatenate(split(jump_all, 2), axis=0))
+    signed = signed_ref[...]
+    plain = jnp.abs(signed)
+    diff_high, diff_low = split(diff_all, 2)
+    jump_high, jump_low = split(jump_all, 2)
+    total = total + (mm(signed, diff_high) + mm(signed, diff_low))
+    spread = mm(plain, jump_high) + mm(plain, jump_low)
 
     for c in copies_c:
         c.wait()
@@ -243,7 +249,7 @@
 
     lane = lax.broadcasted_iota(jnp.int32, (1, count), 1)
     part = lane // width
-    new = []
+    new, halo = [], []
     extra = jnp.zeros((FPAD, count), F32)
     for v in range(NV):
         cols = slice(v * count, (v + 1) * count)
@@ -256,17 +262,21 @@
             packed_tail = jnp.where(part == (3 + g) % 4, turned, packed_tail)
         head[v * FPAD : (v + 1) * FPAD, :] = packed_head
         tail[v * FPAD : (v + 1) * FPAD, :] = packed_tail
+        at = pl.ds(v * FPAD, FPAD)
+        for i, (src, dst, t) in enumerate(((tail, got_tail, 1), (head, got_head, -1))):
+            k = 2 * v + i
+            c = remote(src.at[at], dst.at[at], halo_send.at[k], halo_recv.at[k], on_curve(t))
+            c.start()
+            halo.append(c)
         last = pltpu.roll(x[3 * FPAD :], (v - (count - width - 1)) % count, 1)
         extra = jnp.where(lane == v, last, extra)
     tail[NV * FPAD :, :] = extra
-    halo = [
-        remote(tail, got_tail, halo_send.at[0], halo_recv.at[0], on_curve(1)),
-        remote(head, got_head, halo_send.at[1], halo_recv.at[1], on_curve(-1)),
-    ]
-    for c in halo:
-        c.start()
-
-    shift = ints[7:8]
+    at = pl.ds(NV * FPAD, FPAD)
+    c = remote(tail.at[at], got_tail.at[at], halo_send.at[2 * NV], halo_recv.at[2 * NV], on_curve(1))
+    c.start()
+    halo.append(c)
+
+    shift = shifts_ref[0, 0]
 
     def chosen(start):
         q = start + lane
@@ -275,12 +285,11 @@
 
     hot, foreign = chosen(shift)
     hot_before, foreign_before = chosen(shift - 1)
-    for c in halo:
-        c.wait()
-
-    rows, rows_before = [], []
-    extra = got_tail[NV * FPAD :, :]
+    corners = []
     for v in range(NV):
+        halo[2 * v].wait()
+        halo[2 * v + 1].wait()
+        rows = []
         below = got_tail[v * FPAD : (v + 1) * FPAD, :]
         above = got_head[v * FPAD : (v + 1) * FPAD, :]
         for g in range(4):
@@ -289,12 +298,16 @@
                 ends = pltpu.roll(ends, count - g * width, 1)
             own = new[v][g * FPAD : (g + 1) * FPAD]
             rows.append(jnp.where(foreign, ends, own))
+        corners.append((ends, own))
+        moved_ref[v] = pick(jnp.concatenate(rows, axis=0), hot)[:NODES]
+    halo[2 * NV].wait()
+    rows_before = []
+    extra = got_tail[NV * FPAD :, :]
+    for v in range(NV):
+        ends, own = corners[v]
         last = pltpu.roll(extra, count - width - 1 - v, 1)
         ends = jnp.where(lane == count - width - 1, last, ends)
         rows_before.append(jnp.where(foreign_before, ends, own))
-    out = pick(jnp.concatenate(rows, axis=0), hot)
-    for v in range(NV):
-        moved_ref[v] = out[v * NPAD : v * NPAD + NODES]
     upper_ref[...] = pick(jnp.concatenate(rows_before, axis=0), hot_before)
 
     skip = NODES - FACE - 3 * FPAD
@@ -310,14 +323,7 @@
     padded = jnp.pad(
         state.reshape(NV, NODES, count), ((0, 0), (0, NPAD - NODES), (0, 0)), constant_values=1.0
     )
-    local = neighbours.reshape(6, count)
-    elsewhere = (local // count % n_curve != lax.axis_index("curve")).astype(jnp.int32) * count
-    face = jnp.arange(6, dtype=jnp.int32)[:, None]
-    slot = local % count + jnp.where(face >= 4, elsewhere, 0)
-    ints = jnp.concatenate(
-        [slot, levels.reshape(1, count), jnp.broadcast_to(shifts.reshape(1, 1), (1, count))], axis=0
-    )
-    div, signed, plain = matrices()
+    div, signed = matrices()
     vmem = pl.BlockSpec(memory_space=pltpu.VMEM)
     moved, mortar = pl.pallas_call(
         functools.partial(kernel, n_curve, n_slab),
@@ -325,7 +331,7 @@
             jax.ShapeDtypeStruct((NV, NODES, count), F32),
             jax.ShapeDtypeStruct((NV, FACE, count), F32),
         ),
-        in_specs=[vmem] * 5,
+        in_specs=[vmem] * 3 + [pl.BlockSpec(memory_space=pltpu.SMEM)] + [vmem] * 2,
         out_specs=(vmem, vmem),
         scratch_shapes=[
             pltpu.VMEM((6, NV * FPAD, count), F32),
@@ -345,14 +351,14 @@
             pltpu.SemaphoreType.DMA((n_slab - 1,)),
             pltpu.SemaphoreType.DMA((n_curve - 1,)),
             pltpu.SemaphoreType.DMA((n_curve - 1,)),
-            pltpu.SemaphoreType.DMA((2,)),
-            pltpu.SemaphoreType.DMA((2,)),
+            pltpu.SemaphoreType.DMA((2 * NV + 1,)),
+            pltpu.SemaphoreType.DMA((2 * NV + 1,)),
         ],
         compiler_params=pltpu.CompilerParams(
             collective_id=0, has_side_effects=True, vmem_limit_bytes=32 * 1024 * 1024
         ),
         name="substep",
-    )(padded, ints, jnp.asarray(div), jnp.asarray(signed), jnp.asarray(plain))
+    )(padded, levels, neighbours, shifts, jnp.asarray(div), jnp.asarray(signed))
     return moved.reshape(NV, NODES, 1, count), mortar.reshape(NV, FACE, 1, count)
 
 

time: 25.9 us -> 24.6 us (0.950)
  local copies, waits for them, and re-layouts: 4.99 us -> 3.64 us
  Pallas kernels: 19.2 us -> 19.5 us
    unnamed x13 -> x11, local copies, waits for them, and re-layouts: 4.89 us -> 3.62 us
where the time goes in v2:
time: 24.6 us; the launch traced here: 24.4 us
  Pallas kernels  19.5 us (79%)
  local copies, waits for them, and re-layouts  3.64 us (15%)
  between operations  1.33 us (5%)
    pallas_call x1, Pallas kernels, on_device(): pl.pallas_call(functools.partial(kernel, n_curve, n_slab), out_shape=(jax...  19.5 us
    unnamed x11, local copies, waits for them, and re-layouts  3.62 us

profile of v2, /device:TPU:0, one launch (start us, length us, event | category | flops | bytes accessed | tf_op | source)
XLA Modules:
  0.0 24.4 jit_solution(14469663463788604534)
XLA Ops:
  1.3 1.0 %copy.12 = f32[5,125,1,128]{3,1,2,0:T(8,128)S(1)} copy(f32[5,125,1,128]{3,2,1,0:T(1,128)} %param.6) | data formatting | bytes 640000
  2.3 0.0 copy-start
  2.3 0.0 copy-start.1
  2.3 0.0 copy-start.2
  2.3 0.0 copy-start.3
  2.4 0.8 %copy-done = bf16[128,768]{1,0:T(8,128)(2,1)S(1)} copy-done((bf16[128,768]{1,0:T(8,128)(2,1)S(1)}, bf16[128,768]{1,0:T(8,128)(2,1)}, u32[]{:S(2)}) %copy-start) | copy-done | bytes 196632
  3.2 0.0 copy-done.1
  3.2 0.0 copy-done.2
  3.2 0.0 copy-done.3
  3.2 19.5 %substep.1 = (f32[5,125,128]{2,1,0:T(8,128)S(1)}, f32[5,25,128]{2,1,0:T(8,128)S(1)}) custom-call(f32[5,128,128]{2,1,0:T(8,128)S(1)} %pad.4.state_ref, s32[1,128]{1,0:T(1,128)S(1)} %copy-done.3, s32[6,1,128]{2,1,0:T(1,128)S(1)} %copy-done.2, s32[1,1]{1,0:T(1,128)S(6)} %copy.13.shifts_ref, bf16[128,768]{1,0:T(8,128)(2,1)S(1)} %copy-done, ...), custom_call_target="tpu_custom_call" | custom-call | tf_op jit(solution)/shard_map/substep/pallas_call | solution.py:328
  22.7 1.1 %copy.8 = f32[5,125,1,128]{3,2,1,0:T(1,128)} copy(f32[5,125,1,128]{3,1,0,2:T(8,128)S(1)} %bitcast.5) | data formatting | bytes 640000
  23.8 0.7 %copy.9 = f32[5,25,1,128]{3,2,1,0:T(1,128)} copy(f32[5,25,1,128]{3,1,0,2:T(8,128)S(1)} %bitcast.6) | data formatting | bytes 128000
  (1 shorter events, 0.0 us)
Async XLA Ops:
  2.3 0.9 %copy-start = (bf16[128,768]{1,0:T(8,128)(2,1)S(1)}, bf16[128,768]{1,0:T(8,128)(2,1)}, u32[]{:S(2)}) copy-start(bf16[128,768]{1,0:T(8,128)(2,1)} %constant.6.clone.div_ref) | copy-start | bytes 589828
  2.3 0.9 %copy-start.1 = (bf16[128,192]{1,0:T(8,128)(2,1)S(1)}, bf16[128,192]{1,0:T(8,128)(2,1)}, u32[]{:S(2)}) copy-start(bf16[128,192]{1,0:T(8,128)(2,1)} %constant.7.clone.signed_ref) | copy-start | bytes 147460
  2.3 0.9 %copy-start.2 = (s32[6,1,128]{2,1,0:T(1,128)S(1)}, s32[6,1,128]{2,1,0:T(1,128)}, u32[]{:S(2)}) copy-start(s32[6,1,128]{2,1,0:T(1,128)} %neighbours_ref.1) | copy-start | bytes 9220
  2.3 0.9 %copy-start.3 = (s32[1,128]{1,0:T(1,128)S(1)}, s32[1,128]{1,0:T(1,128)}, u32[]{:S(2)}) copy-start(s32[1,128]{1,0:T(1,128)} %levels_ref.1) | copy-start | bytes 1540

commit v3 on v2

--- a/solution.py
+++ b/solution.py
@@ -104,8 +104,8 @@
 
 def pick(x, chosen):
     rows = x.shape[0]
-    y = mm(jnp.concatenate(split(x, 3), axis=0), chosen)
-    return y[:rows] + y[rows : 2 * rows] + y[2 * rows :]
+    y = mm(jnp.concatenate(split(x, 2), axis=0), chosen)
+    return y[:rows] + y[rows:]
 
 
 def one_hot(rows, index):

time: 24.6 us -> 24.5 us (level)
  no operation moved by 1% of the time
where the time goes in v3:
time: 24.5 us; the launch traced here: 24.3 us
  Pallas kernels  19.4 us (79%)
  local copies, waits for them, and re-layouts  3.64 us (15%)
  between operations  1.33 us (5%)
    pallas_call x1, Pallas kernels, on_device(): pl.pallas_call(functools.partial(kernel, n_curve, n_slab), out_shape=(jax...  19.4 us
    unnamed x11, local copies, waits for them, and re-layouts  3.62 us

profile of v3, /device:TPU:0, one launch (start us, length us, event | category | flops | bytes accessed | tf_op | source)
XLA Modules:
  0.0 24.3 jit_solution(6463014521116450348)
XLA Ops:
  1.3 1.0 %copy.12 = f32[5,125,1,128]{3,1,2,0:T(8,128)S(1)} copy(f32[5,125,1,128]{3,2,1,0:T(1,128)} %param.6) | data formatting | bytes 640000
  2.3 0.0 copy-start
  2.3 0.0 copy-start.1
  2.3 0.0 copy-start.2
  2.3 0.0 copy-start.3
  2.4 0.8 %copy-done = bf16[128,768]{1,0:T(8,128)(2,1)S(1)} copy-done((bf16[128,768]{1,0:T(8,128)(2,1)S(1)}, bf16[128,768]{1,0:T(8,128)(2,1)}, u32[]{:S(2)}) %copy-start) | copy-done | bytes 196632
  3.2 0.0 copy-done.1
  3.2 0.0 copy-done.2
  3.2 0.0 copy-done.3
  3.2 19.4 %substep.1 = (f32[5,125,128]{2,1,0:T(8,128)S(1)}, f32[5,25,128]{2,1,0:T(8,128)S(1)}) custom-call(f32[5,128,128]{2,1,0:T(8,128)S(1)} %pad.4.state_ref, s32[1,128]{1,0:T(1,128)S(1)} %copy-done.3, s32[6,1,128]{2,1,0:T(1,128)S(1)} %copy-done.2, s32[1,1]{1,0:T(1,128)S(6)} %copy.13.shifts_ref, bf16[128,768]{1,0:T(8,128)(2,1)S(1)} %copy-done, ...), custom_call_target="tpu_custom_call" | custom-call | tf_op jit(solution)/shard_map/substep/pallas_call | solution.py:328
  22.6 1.1 %copy.8 = f32[5,125,1,128]{3,2,1,0:T(1,128)} copy(f32[5,125,1,128]{3,1,0,2:T(8,128)S(1)} %bitcast.5) | data formatting | bytes 640000
  23.6 0.7 %copy.9 = f32[5,25,1,128]{3,2,1,0:T(1,128)} copy(f32[5,25,1,128]{3,1,0,2:T(8,128)S(1)} %bitcast.6) | data formatting | bytes 128000
  (1 shorter events, 0.0 us)
Async XLA Ops:
  2.3 0.9 %copy-start = (bf16[128,768]{1,0:T(8,128)(2,1)S(1)}, bf16[128,768]{1,0:T(8,128)(2,1)}, u32[]{:S(2)}) copy-start(bf16[128,768]{1,0:T(8,128)(2,1)} %constant.6.clone.div_ref) | copy-start | bytes 589828
  2.3 0.9 %copy-start.1 = (bf16[128,192]{1,0:T(8,128)(2,1)S(1)}, bf16[128,192]{1,0:T(8,128)(2,1)}, u32[]{:S(2)}) copy-start(bf16[128,192]{1,0:T(8,128)(2,1)} %constant.7.clone.signed_ref) | copy-start | bytes 147460
  2.3 0.9 %copy-start.2 = (s32[6,1,128]{2,1,0:T(1,128)S(1)}, s32[6,1,128]{2,1,0:T(1,128)}, u32[]{:S(2)}) copy-start(s32[6,1,128]{2,1,0:T(1,128)} %neighbours_ref.1) | copy-start | bytes 9220
  2.3 0.9 %copy-start.3 = (s32[1,128]{1,0:T(1,128)S(1)}, s32[1,128]{1,0:T(1,128)}, u32[]{:S(2)}) copy-start(s32[1,128]{1,0:T(1,128)} %levels_ref.1) | copy-start | bytes 1540

commit v4 on v2

--- a/solution.py
+++ b/solution.py
@@ -249,7 +249,7 @@
 
     lane = lax.broadcasted_iota(jnp.int32, (1, count), 1)
     part = lane // width
-    new, halo = [], []
+    new = []
     extra = jnp.zeros((FPAD, count), F32)
     for v in range(NV):
         cols = slice(v * count, (v + 1) * count)
@@ -262,19 +262,15 @@
             packed_tail = jnp.where(part == (3 + g) % 4, turned, packed_tail)
         head[v * FPAD : (v + 1) * FPAD, :] = packed_head
         tail[v * FPAD : (v + 1) * FPAD, :] = packed_tail
-        at = pl.ds(v * FPAD, FPAD)
-        for i, (src, dst, t) in enumerate(((tail, got_tail, 1), (head, got_head, -1))):
-            k = 2 * v + i
-            c = remote(src.at[at], dst.at[at], halo_send.at[k], halo_recv.at[k], on_curve(t))
-            c.start()
-            halo.append(c)
         last = pltpu.roll(x[3 * FPAD :], (v - (count - width - 1)) % count, 1)
         extra = jnp.where(lane == v, last, extra)
     tail[NV * FPAD :, :] = extra
-    at = pl.ds(NV * FPAD, FPAD)
-    c = remote(tail.at[at], got_tail.at[at], halo_send.at[2 * NV], halo_recv.at[2 * NV], on_curve(1))
-    c.start()
-    halo.append(c)
+    halo = [
+        remote(tail, got_tail, halo_send.at[0], halo_recv.at[0], on_curve(1)),
+        remote(head, got_head, halo_send.at[1], halo_recv.at[1], on_curve(-1)),
+    ]
+    for c in halo:
+        c.start()
 
     shift = shifts_ref[0, 0]
 
@@ -285,11 +281,12 @@
 
     hot, foreign = chosen(shift)
     hot_before, foreign_before = chosen(shift - 1)
-    corners = []
+    for c in halo:
+        c.wait()
+
+    rows, rows_before = [], []
+    extra = got_tail[NV * FPAD :, :]
     for v in range(NV):
-        halo[2 * v].wait()
-        halo[2 * v + 1].wait()
-        rows = []
         below = got_tail[v * FPAD : (v + 1) * FPAD, :]
         above = got_head[v * FPAD : (v + 1) * FPAD, :]
         for g in range(4):
@@ -298,16 +295,12 @@
                 ends = pltpu.roll(ends, count - g * width, 1)
             own = new[v][g * FPAD : (g + 1) * FPAD]
             rows.append(jnp.where(foreign, ends, own))
-        corners.append((ends, own))
-        moved_ref[v] = pick(jnp.concatenate(rows, axis=0), hot)[:NODES]
-    halo[2 * NV].wait()
-    rows_before = []
-    extra = got_tail[NV * FPAD :, :]
-    for v in range(NV):
-        ends, own = corners[v]
         last = pltpu.roll(extra, count - width - 1 - v, 1)
         ends = jnp.where(lane == count - width - 1, last, ends)
         rows_before.append(jnp.where(foreign_before, ends, own))
+    out = pick(jnp.concatenate(rows, axis=0), hot)
+    for v in range(NV):
+        moved_ref[v] = out[v * NPAD : v * NPAD + NODES]
     upper_ref[...] = pick(jnp.concatenate(rows_before, axis=0), hot_before)
 
     skip = NODES - FACE - 3 * FPAD
@@ -351,8 +344,8 @@
             pltpu.SemaphoreType.DMA((n_slab - 1,)),
             pltpu.SemaphoreType.DMA((n_curve - 1,)),
             pltpu.SemaphoreType.DMA((n_curve - 1,)),
-            pltpu.SemaphoreType.DMA((2 * NV + 1,)),
-            pltpu.SemaphoreType.DMA((2 * NV + 1,)),
+            pltpu.SemaphoreType.DMA((2,)),
+            pltpu.SemaphoreType.DMA((2,)),
         ],
         compiler_params=pltpu.CompilerParams(
             collective_id=0, has_side_effects=True, vmem_limit_bytes=32 * 1024 * 1024

time: 24.6 us -> 24.4 us (level)
  Pallas kernels: 19.5 us -> 19.2 us
where the time goes in v4:
time: 24.4 us; the launch traced here: 24.2 us
  Pallas kernels  19.2 us (79%)
  local copies, waits for them, and re-layouts  3.64 us (15%)
  between operations  1.33 us (5%)
    pallas_call x1, Pallas kernels, on_device(): pl.pallas_call(functools.partial(kernel, n_curve, n_slab), out_shape=(jax...  19.2 us
    unnamed x11, local copies, waits for them, and re-layouts  3.62 us

profile of v4, /device:TPU:0, one launch (start us, length us, event | category | flops | bytes accessed | tf_op | source)
XLA Modules:
  0.0 24.2 jit_solution(15045786508106722971)
XLA Ops:
  1.3 1.0 %copy.12 = f32[5,125,1,128]{3,1,2,0:T(8,128)S(1)} copy(f32[5,125,1,128]{3,2,1,0:T(1,128)} %param.6) | data formatting | bytes 640000
  2.3 0.0 copy-start
  2.3 0.0 copy-start.1
  2.3 0.0 copy-start.2
  2.3 0.0 copy-start.3
  2.4 0.8 %copy-done = bf16[128,768]{1,0:T(8,128)(2,1)S(1)} copy-done((bf16[128,768]{1,0:T(8,128)(2,1)S(1)}, bf16[128,768]{1,0:T(8,128)(2,1)}, u32[]{:S(2)}) %copy-start) | copy-done | bytes 196632
  3.2 0.0 copy-done.1
  3.2 0.0 copy-done.2
  3.2 0.0 copy-done.3
  3.2 19.2 %substep.1 = (f32[5,125,128]{2,1,0:T(8,128)S(1)}, f32[5,25,128]{2,1,0:T(8,128)S(1)}) custom-call(f32[5,128,128]{2,1,0:T(8,128)S(1)} %pad.4.state_ref, s32[1,128]{1,0:T(1,128)S(1)} %copy-done.3, s32[6,1,128]{2,1,0:T(1,128)S(1)} %copy-done.2, s32[1,1]{1,0:T(1,128)S(6)} %copy.13.shifts_ref, bf16[128,768]{1,0:T(8,128)(2,1)S(1)} %copy-done, ...), custom_call_target="tpu_custom_call" | custom-call | tf_op jit(solution)/shard_map/substep/pallas_call | solution.py:321
  22.5 1.1 %copy.8 = f32[5,125,1,128]{3,2,1,0:T(1,128)} copy(f32[5,125,1,128]{3,1,0,2:T(8,128)S(1)} %bitcast.5) | data formatting | bytes 640000
  23.5 0.7 %copy.9 = f32[5,25,1,128]{3,2,1,0:T(1,128)} copy(f32[5,25,1,128]{3,1,0,2:T(8,128)S(1)} %bitcast.6) | data formatting | bytes 128000
  (1 shorter events, 0.0 us)
Async XLA Ops:
  2.3 0.9 %copy-start = (bf16[128,768]{1,0:T(8,128)(2,1)S(1)}, bf16[128,768]{1,0:T(8,128)(2,1)}, u32[]{:S(2)}) copy-start(bf16[128,768]{1,0:T(8,128)(2,1)} %constant.6.clone.div_ref) | copy-start | bytes 589828
  2.3 0.9 %copy-start.1 = (bf16[128,192]{1,0:T(8,128)(2,1)S(1)}, bf16[128,192]{1,0:T(8,128)(2,1)}, u32[]{:S(2)}) copy-start(bf16[128,192]{1,0:T(8,128)(2,1)} %constant.7.clone.signed_ref) | copy-start | bytes 147460
  2.3 0.9 %copy-start.2 = (s32[6,1,128]{2,1,0:T(1,128)S(1)}, s32[6,1,128]{2,1,0:T(1,128)}, u32[]{:S(2)}) copy-start(s32[6,1,128]{2,1,0:T(1,128)} %neighbours_ref.1) | copy-start | bytes 9220
  2.3 0.9 %copy-start.3 = (s32[1,128]{1,0:T(1,128)S(1)}, s32[1,128]{1,0:T(1,128)}, u32[]{:S(2)}) copy-start(s32[1,128]{1,0:T(1,128)} %levels_ref.1) | copy-start | bytes 1540

commit v5 on v4

--- a/solution.py
+++ b/solution.py
@@ -158,6 +158,16 @@
                 n = 100 * (f - 4)
                 faces[f, r : r + FACE, :] = state_ref[v, n : n + FACE, :]
 
+    pl.semaphore_wait(barrier, n_slab + n_curve - 2)
+    copies_f = [
+        remote(faces.at[5], got.at[2], face_send.at[2], face_recv.at[2], on_curve(1)),
+        remote(faces.at[4], got.at[3], face_send.at[3], face_recv.at[3], on_curve(-1)),
+        remote(faces.at[1], got.at[0], face_send.at[0], face_recv.at[0], on_slab(1)),
+        remote(faces.at[0], got.at[1], face_send.at[1], face_recv.at[1], on_slab(-1)),
+    ]
+    for c in copies_f[:2]:
+        c.start()
+
     u = [state_ref[v] for v in range(NV)]
     inv, vel, press = primitive(u)
     speed = jnp.sqrt(vel[0] * vel[0] + vel[1] * vel[1] + vel[2] * vel[2]) + jnp.sqrt(GAMMA * press * inv)
@@ -167,19 +177,12 @@
     row8 = lax.broadcasted_iota(jnp.int32, (8, count), 0)
     mine_s[...] = jnp.where(row8 == 0, fastest, fastest * scale)
 
-    pl.semaphore_wait(barrier, n_slab + n_curve - 2)
     copies_s = []
     for t in range(1, n_slab):
         c = remote(mine_s, from_s.at[t - 1], s_send.at[t - 1], s_recv.at[t - 1], on_slab(t))
         c.start()
         copies_s.append(c)
-    copies_f = [
-        remote(faces.at[5], got.at[2], face_send.at[2], face_recv.at[2], on_curve(1)),
-        remote(faces.at[4], got.at[3], face_send.at[3], face_recv.at[3], on_curve(-1)),
-        remote(faces.at[1], got.at[0], face_send.at[0], face_recv.at[0], on_slab(1)),
-        remote(faces.at[0], got.at[1], face_send.at[1], face_recv.at[1], on_slab(-1)),
-    ]
-    for c in copies_f:
+    for c in copies_f[2:]:
         c.start()
 
     blocks = []

time: 24.4 us -> 24.6 us (level)
  no operation moved by 1% of the time
where the time goes in v5:
time: 24.6 us; the launch traced here: 24.4 us
  Pallas kernels  19.4 us (79%)
  local copies, waits for them, and re-layouts  3.64 us (15%)
  between operations  1.33 us (5%)
    pallas_call x1, Pallas kernels, on_device(): pl.pallas_call(functools.partial(kernel, n_curve, n_slab), out_shape=(jax...  19.4 us
    unnamed x11, local copies, waits for them, and re-layouts  3.62 us

profile of v5, /device:TPU:0, one launch (start us, length us, event | category | flops | bytes accessed | tf_op | source)
XLA Modules:
  0.0 24.4 jit_solution(17771202078790179577)
XLA Ops:
  1.3 1.0 %copy.12 = f32[5,125,1,128]{3,1,2,0:T(8,128)S(1)} copy(f32[5,125,1,128]{3,2,1,0:T(1,128)} %param.6) | data formatting | bytes 640000
  2.3 0.0 copy-start
  2.3 0.0 copy-start.1
  2.3 0.0 copy-start.2
  2.3 0.0 copy-start.3
  2.4 0.8 %copy-done = bf16[128,768]{1,0:T(8,128)(2,1)S(1)} copy-done((bf16[128,768]{1,0:T(8,128)(2,1)S(1)}, bf16[128,768]{1,0:T(8,128)(2,1)}, u32[]{:S(2)}) %copy-start) | copy-done | bytes 196632
  3.2 0.0 copy-done.1
  3.2 0.0 copy-done.2
  3.2 0.0 copy-done.3
  3.2 19.4 %substep.1 = (f32[5,125,128]{2,1,0:T(8,128)S(1)}, f32[5,25,128]{2,1,0:T(8,128)S(1)}) custom-call(f32[5,128,128]{2,1,0:T(8,128)S(1)} %pad.4.state_ref, s32[1,128]{1,0:T(1,128)S(1)} %copy-done.3, s32[6,1,128]{2,1,0:T(1,128)S(1)} %copy-done.2, s32[1,1]{1,0:T(1,128)S(6)} %copy.13.shifts_ref, bf16[128,768]{1,0:T(8,128)(2,1)S(1)} %copy-done, ...), custom_call_target="tpu_custom_call" | custom-call | tf_op jit(solution)/shard_map/substep/pallas_call | solution.py:324
  22.7 1.1 %copy.8 = f32[5,125,1,128]{3,2,1,0:T(1,128)} copy(f32[5,125,1,128]{3,1,0,2:T(8,128)S(1)} %bitcast.5) | data formatting | bytes 640000
  23.7 0.7 %copy.9 = f32[5,25,1,128]{3,2,1,0:T(1,128)} copy(f32[5,25,1,128]{3,1,0,2:T(8,128)S(1)} %bitcast.6) | data formatting | bytes 128000
  (1 shorter events, 0.0 us)
Async XLA Ops:
  2.3 0.9 %copy-start = (bf16[128,768]{1,0:T(8,128)(2,1)S(1)}, bf16[128,768]{1,0:T(8,128)(2,1)}, u32[]{:S(2)}) copy-start(bf16[128,768]{1,0:T(8,128)(2,1)} %constant.6.clone.div_ref) | copy-start | bytes 589828
  2.3 0.9 %copy-start.1 = (bf16[128,192]{1,0:T(8,128)(2,1)S(1)}, bf16[128,192]{1,0:T(8,128)(2,1)}, u32[]{:S(2)}) copy-start(bf16[128,192]{1,0:T(8,128)(2,1)} %constant.7.clone.signed_ref) | copy-start | bytes 147460
  2.3 0.9 %copy-start.2 = (s32[6,1,128]{2,1,0:T(1,128)S(1)}, s32[6,1,128]{2,1,0:T(1,128)}, u32[]{:S(2)}) copy-start(s32[6,1,128]{2,1,0:T(1,128)} %neighbours_ref.1) | copy-start | bytes 9220
  2.3 0.9 %copy-start.3 = (s32[1,128]{1,0:T(1,128)S(1)}, s32[1,128]{1,0:T(1,128)}, u32[]{:S(2)}) copy-start(s32[1,128]{1,0:T(1,128)} %levels_ref.1) | copy-start | bytes 1540
